TPU v7x, 512 devices: a whole 4x4x16 slice. The times are simulated.
512 devices in a mesh: rep: 64 (over z, y_lo, core), tp: 8 (over y_hi, x).
Axes of the slice: x: 4, y: 4 (y_hi: 2, y_lo: 2; y = y_hi * 2 + y_lo), z: 16, core: 2. Of those that a mesh axis runs over, the one named last changes fastest.
Arguments:
- hidden_rows: bfloat16 [64, 2, 256, 2048], P('rep', None, 'tp'), may hold values from -6 to 6
- query_heads: bfloat16 [64, 2, 256, 2048], P('rep', None, None, 'tp'), may hold values from -6 to 6
- key_heads: bfloat16 [64, 2, 256, 2048], P('rep', None, None, 'tp'), may hold values from -6 to 6
- teacher_out: bfloat16 [64, 2, 256, 2048], P('rep', None, None, 'tp'), may hold values from -6 to 6
- segment_ids: int32 [64, 2, 256], P('rep'), may hold values from 0 to 7, never falling along the last dimension, each value on 1 to 64 neighbouring positions
- prompt_lens: int32 [64, 2, 8], P('rep'), may hold values from 0 to 31
- gossip_step: int32 [1], replicated, may hold values from 0 to 63
- value_weight: bfloat16 [64, 2048, 2048], P('rep', None, 'tp'), may hold values from -0.125 to 0.125
- momentum: bfloat16 [64, 2048, 2048], P('rep', None, 'tp'), may hold values from -0.29882812 to 0.29882812
Outputs:
- new_weight: bfloat16 [64, 2048, 2048], P('rep', None, 'tp')
- new_momentum: bfloat16 [64, 2048, 2048], P('rep', None, 'tp')
Inputs may be any that keep to these rules, and one draw needn't show every extreme that they name: `segment_ids`: ids never fall along the 256 positions; each microbatch holds 1 to 64 positions, and one of each pack exactly 64. `gossip_step`: the same for every replica.
All inputs are finite; a program needn't handle non-finite values.
Results may differ from a plain program's by a relative error of at most 0.013.
Values may be sent and summed in bfloat16 or wider, within the bound.
A program may use at most 64 MiB of HBM per device.

v0:
```python
import functools
import math

import jax
import jax.numpy as jnp
from jax import lax
from jax.experimental import pallas as pl
from jax.experimental.pallas import tpu as pltpu
from jax.sharding import PartitionSpec as P

HEAD_DIM = 128
LEARN_RATE = 0.1
MOMENTUM_DECAY = 0.9
LEVELS = 6
TOK = 256
ROWS = 2048
COLS = 256
TP = 8
SHARD = TOK // TP
HALF = ROWS // 2
CHUNKS = 8
CROWS = ROWS // CHUNKS
F32 = jnp.float32
BF16 = jnp.bfloat16
MESH = pl.DeviceIdType.MESH


def remote(src, dst, send, recv, device):
    return pltpu.make_async_remote_copy(
        src_ref=src, dst_ref=dst, send_sem=send, recv_sem=recv, device_id=device, device_id_type=MESH
    )


def partner_of(rep, bit):
    size = 1 << bit
    return rep + size * (1 - 2 * ((rep // size) % 2))


def kernel(
    bit_a, bit_b,
    hid, qry, key, tea, seg, prm, wgt, mom,
    w_out, m_out,
    x, qv, kv, tv, segv, prmv, wv, mv, stepped, landed, held, att, att_t, live, dvals, total,
    load_sem, x_send, x_recv, g_send, g_recv, low_send, low_recv, out_sem,
):
    early = bit_a <= 2
    lean = bit_a <= 1
    rep = lax.axis_index("rep")
    tp = lax.axis_index("tp")
    row = (tp // 4) * 4
    right = row + (tp + 1) % 4
    left = row + (tp + 3) % 4
    cross = (tp + 4) % 8
    far = row + (tp + 2) % 4
    cross_right = (right + 4) % 8
    cross_left = (left + 4) % 8
    to_right = (rep, right)
    to_left = (rep, left)
    to_cross = (rep, cross)
    peers = ((partner_of(rep, bit_a), tp), (partner_of(rep, bit_b), tp))

    own_load = [pltpu.make_async_copy(hid.at[0, s], x.at[s, tp], load_sem.at[s]) for s in range(2)]
    loads = [
        pltpu.make_async_copy(seg.at[0], segv, load_sem.at[2]),
        pltpu.make_async_copy(prm.at[0], prmv, load_sem.at[3]),
        pltpu.make_async_copy(qry.at[0], qv, load_sem.at[4]),
        pltpu.make_async_copy(key.at[0], kv, load_sem.at[5]),
        pltpu.make_async_copy(tea.at[0], tv, load_sem.at[6]),
        pltpu.make_async_copy(wgt.at[0], wv, load_sem.at[7]),
        pltpu.make_async_copy(mom.at[0], mv, load_sem.at[8]),
    ]
    for copy in own_load + loads:
        copy.start()

    barrier = pltpu.get_barrier_semaphore()
    for device in (to_right, to_left, to_cross) + peers:
        pl.semaphore_signal(barrier, inc=1, device_id=device, device_id_type=MESH)
    pl.semaphore_wait(barrier, 5)

    route = (
        (tp, to_right, 0),
        (tp, to_left, 1),
        (tp, to_cross, 0),
        (tp, to_cross, 1),
        (tp, to_right, 1),
        (tp, to_left, 0),
        (left, to_right, 0),
        (right, to_left, 1),
        (cross, to_right, 0),
        (cross, to_left, 0),
        (cross, to_right, 1),
        (cross, to_left, 1),
        (far, to_cross, 0),
        (far, to_cross, 1),
    )

    lean_route = route[:12] + ((cross_left, to_right, 0), (cross_right, to_left, 1))

    def hop(s, n):
        slot, device, half = (lean_route if lean and s else route)[n]
        part = x.at[s, slot, :, pl.ds(half * HALF, HALF)]
        return remote(part, part, x_send.at[s, n], x_recv.at[s, n], device)

    def start(s, *hops):
        for n in hops:
            hop(s, n).start()

    def stage_a(s):
        start(s, 2, 0, 1, 3, 4, 5)

    def stage_b(s):
        for arrived, onward in ((0, (6,)), (1, (7,)), (2, (8, 9)), (3, (10, 11))):
            hop(s, arrived).wait_recv()
            start(s, *onward)

    def stage_c(s):
        for arrived, onward in ((8, 12), (11, 13)) if lean and s else ((6, 12), (7, 13)):
            hop(s, arrived).wait_recv()
            start(s, onward)

    def stage_d(s):
        for n in (4, 5, 6, 7, 9, 10, 12, 13) if lean and s else (4, 5, 8, 9, 10, 11, 12, 13):
            hop(s, n).wait_recv()

    def stage_end(s):
        for n in range(14):
            hop(s, n).wait_send()

    def attention(s):
        ids = jnp.broadcast_to(segv[pl.ds(s, 1), :].astype(F32), (TOK, TOK))
        ids_t = ids.T
        rows = lax.broadcasted_iota(jnp.int32, (TOK, TOK), 0)
        columns = lax.broadcasted_iota(jnp.int32, (TOK, TOK), 1)
        same = ids == ids_t
        allowed = same & (columns <= rows)
        place = jnp.sum(jnp.where(same & (columns < rows), 1.0, 0.0), axis=1, keepdims=True)
        lens = jnp.broadcast_to(prmv[pl.ds(s, 1), :].astype(F32), (TOK, 8))
        labels = lax.broadcasted_iota(jnp.int32, (TOK, 8), 1).astype(F32)
        prompt = jnp.sum(jnp.where(ids_t[:, :8] == labels, lens, 0.0), axis=1, keepdims=True)
        alive = jnp.where(place >= prompt, 1.0, 0.0)
        count = jnp.sum(alive, axis=0, keepdims=True)
        live[s] = jnp.broadcast_to(alive / count, (TOK, 128))
        for h in range(2):
            cut = pl.ds(h * HEAD_DIM, HEAD_DIM)
            scores = lax.dot_general(
                qv[s, :, cut], kv[s, :, cut], (((1,), (1,)), ((), ())), preferred_element_type=F32
            ) / math.sqrt(HEAD_DIM)
            scores = jnp.where(allowed, scores, -jnp.inf)
            top = jnp.max(scores, axis=1, keepdims=True)
            weights = jnp.exp(scores - top)
            soft = weights / jnp.sum(weights, axis=1, keepdims=True)
            att[s, h] = soft.astype(BF16)
            att_t[s, h] = soft.T.astype(BF16)

    def value_grad(s, values):
        parts = []
        for h in range(2):
            cut = slice(h * HEAD_DIM, (h + 1) * HEAD_DIM)
            attended = jnp.dot(att[s, h], values[:, cut], preferred_element_type=F32)
            residue = attended - tv[s, :, cut].astype(F32)
            errors = (residue * live[s]).astype(BF16)
            parts.append(jnp.dot(att_t[s, h], errors, preferred_element_type=F32).astype(BF16))
        return jnp.concatenate(parts, axis=1)

    def send(s, i):
        cut = pl.ds(i * CROWS, CROWS)
        return remote(
            stepped.at[s, cut], landed.at[s, cut], g_send.at[s, i], g_recv.at[s, i], peers[s]
        )

    def out_copy(n, i):
        cut = pl.ds(i * CROWS, CROWS)
        source, target = ((wv, w_out), (mv, m_out))[n]
        return pltpu.make_async_copy(source.at[cut], target.at[0, cut], out_sem.at[n, i])

    def rows_of(i):
        return pl.ds(pl.multiple_of(i * CROWS, CROWS), CROWS)

    def grad_rows(n, i, dvalues):
        lhs = x[n, :, :, rows_of(i)].reshape(TOK, CROWS)
        return lax.dot_general(lhs, dvalues, (((0,), (0,)), ((), ())), preferred_element_type=F32)

    def update(s, i, target):
        cut = rows_of(i)
        moment = (
            MOMENTUM_DECAY * mv[cut, :].astype(F32) + grad_rows(s, i, dvals[s])
        ).astype(BF16)
        mv[cut, :] = moment
        target[cut, :] = (wv[cut, :].astype(F32) - LEARN_RATE * moment.astype(F32)).astype(BF16)

    def average(s, i):
        cut = rows_of(i)
        send(s, i).wait_recv()
        mean = (stepped[s, cut, :].astype(F32) + landed[s, cut, :].astype(F32)) * 0.5
        wv[cut, :] = mean.astype(BF16)

    def add_values(i, count=1):
        cut = pl.ds(pl.multiple_of(i * CROWS, CROWS), count * CROWS)
        total[...] += jnp.dot(
            x[1, :, :, cut].reshape(TOK, count * CROWS), wv[cut, :], preferred_element_type=F32
        )

    def loop(first, last, body):
        def step(i, carry):
            body(i)
            return carry

        lax.fori_loop(first, last, step, 0)

    def first_update(i):
        update(0, i, stepped.at[0])
        send(0, i).start()

    def first_gossip(i):
        average(0, i)
        if early:
            cut = rows_of(i)
            ahead = wv[cut, :].astype(F32) - (LEARN_RATE * MOMENTUM_DECAY) * mv[cut, :].astype(F32)
            stepped[1, cut, :] = ahead.astype(BF16)
            send(1, i).start()

    def first_gossip_values(i):
        first_gossip(i)
        add_values(i)

    def second_update(i):
        if early:
            update(1, i, held)
        else:
            update(1, i, stepped.at[1])
            send(1, i).start()
        out_copy(1, i).start()

    def second_gossip(i):
        if early:
            cut = rows_of(i)
            send(1, i).wait_recv()
            theirs = landed[1, cut, :].astype(F32) - LEARN_RATE * grad_rows(2, i, dvals[2])
            wv[cut, :] = ((held[cut, :].astype(F32) + theirs) * 0.5).astype(BF16)
        else:
            average(1, i)
        out_copy(0, i).start()

    def finish(i):
        for s in range(2):
            send(s, i).wait_send()
            out_copy(s, i).wait()

    if early:
        their_rows = remote(
            hid.at[0, 1], x.at[2, tp], low_send.at[0], low_recv.at[0], peers[1]
        )
        their_grad = remote(dvals.at[1], dvals.at[2], low_send.at[1], low_recv.at[1], peers[1])

    own_load[0].wait()
    stage_a(0)
    if early and bit_b > 1:
        their_rows.start()
    for copy in loads[:5]:
        copy.wait()
    attention(0)
    stage_b(0)
    stage_c(0)
    own_load[1].wait()
    if lean:
        start(1, 2, 3)
        if bit_b == 1:
            their_rows.start()
    attention(1)
    for copy in loads[5:]:
        copy.wait()
    stage_d(0)
    if lean:
        start(1, 0, 1, 4, 5)
        their_rows.wait_recv()
        start(2, 2, 3)
    else:
        stage_a(1)

    values = jnp.dot(
        x[0].reshape(TOK, ROWS), wv[...], preferred_element_type=F32
    ).astype(BF16)
    dvals[0] = value_grad(0, values)
    loop(0, CHUNKS, first_update)
    total[...] = jnp.zeros((TOK, COLS), F32)
    stage_b(1)
    if bit_a == 0:
        loop(0, CHUNKS, first_gossip)
        stage_c(1)
        stage_d(1)
        start(2, 0, 1, 4, 5)
        add_values(0, CHUNKS)
    else:
        stage_c(1)
        if lean:
            start(2, 0, 1, 4, 5)
        elif early:
            their_rows.wait_recv()
            stage_a(2)
        loop(0, 4, first_gossip)
        stage_d(1)
        add_values(0, 4)
        if early:
            stage_b(2)
        loop(4, 6, first_gossip_values)
        if early:
            stage_c(2)
        loop(6, CHUNKS, first_gossip_values)

    dvals[1] = value_grad(1, total[...].astype(BF16))
    if early:
        their_grad.start()
    if bit_a == 0:
        stage_b(2)
    loop(0, CHUNKS, second_update)
    if early:
        if bit_a == 0:
            stage_c(2)
        stage_d(2)
        their_grad.wait_recv()
    loop(0, CHUNKS, second_gossip)
    loop(0, CHUNKS, finish)
    stage_end(0)
    stage_end(1)
    if early:
        stage_end(2)
        their_rows.wait_send()
        their_grad.wait_send()


def fused(bit, *operands):
    hid, qry, key, tea, seg, prm, wgt, mom = operands
    any_space = pl.BlockSpec(memory_space=pl.ANY)
    dma = pltpu.SemaphoreType.DMA
    return pl.pallas_call(
        functools.partial(kernel, bit, (bit + 1) % LEVELS),
        out_shape=(
            jax.ShapeDtypeStruct(wgt.shape, BF16),
            jax.ShapeDtypeStruct(mom.shape, BF16),
        ),
        in_specs=[any_space] * 8,
        out_specs=(any_space, any_space),
        scratch_shapes=[
            pltpu.VMEM((3, TP, SHARD, ROWS), BF16),
            pltpu.VMEM((2, TOK, COLS), BF16),
            pltpu.VMEM((2, TOK, COLS), BF16),
            pltpu.VMEM((2, TOK, COLS), BF16),
            pltpu.VMEM((2, TOK), jnp.int32),
            pltpu.VMEM((2, 8), jnp.int32),
            pltpu.VMEM((ROWS, COLS), BF16),
            pltpu.VMEM((ROWS, COLS), BF16),
            pltpu.VMEM((2, ROWS, COLS), BF16),
            pltpu.VMEM((2, ROWS, COLS), BF16),
            pltpu.VMEM((ROWS, COLS), BF16),
            pltpu.VMEM((2, 2, TOK, TOK), BF16),
            pltpu.VMEM((2, 2, TOK, TOK), BF16),
            pltpu.VMEM((2, TOK, 128), F32),
            pltpu.VMEM((3, TOK, COLS), BF16),
            pltpu.VMEM((TOK, COLS), F32),
            dma((9,)),
            dma((3, 14)),
            dma((3, 14)),
            dma((2, CHUNKS)),
            dma((2, CHUNKS)),
            dma((2,)),
            dma((2,)),
            dma((2, CHUNKS)),
        ],
        compiler_params=pltpu.CompilerParams(
            collective_id=bit, has_side_effects=True, vmem_limit_bytes=56 * 1024 * 1024
        ),
        name=f"gossip_{bit}",
    )(*operands)


def per_device(hid, qry, key, tea, seg, prm, gossip_step, wgt, mom):
    bit = gossip_step[0] % LEVELS
    branches = [functools.partial(fused, level) for level in range(LEVELS)]
    return lax.switch(bit, branches, hid, qry, key, tea, seg, prm, wgt, mom)


def solution(mesh):
    in_specs = (
        P("rep", None, "tp", None),
        P("rep", None, None, "tp"),
        P("rep", None, None, "tp"),
        P("rep", None, None, "tp"),
        P("rep", None, None),
        P("rep", None, None),
        P(),
        P("rep", None, "tp"),
        P("rep", None, "tp"),
    )
    out_specs = (P("rep", None, "tp"), P("rep", None, "tp"))
    return jax.shard_map(
        per_device, mesh=mesh, in_specs=in_specs, out_specs=out_specs, check_vma=False
    )
```

profile of v0, /device:TPU:128, one launch (start us, length us, event | category | flops | bytes accessed | tf_op | source)
XLA Modules:
  0.0 85.4 jit_solution(1440884553826260939)
XLA Ops:
  1.3 0.0 copy-start
  1.3 0.0 copy-start.1
  1.3 0.7 copy-done
  2.0 0.0 copy-done.1
  2.0 81.4 %conditional.1 = ((bf16[1,2048,256]{2,1,0:T(8,128)(2,1)S(1)}, bf16[1,2048,256]{2,1,0:T(8,128)(2,1)S(1)})) conditional(s32[]{:T(128)} %clamp.3, (bf16[1,2,32,2048]{3,2,1,0:T(8,128)(2,1)}, bf16[1,2,256,256]{3,2,1,0:T(8,128)(2,1)}, bf16[1,2,256,256]{3,2,1,0:T(8,128)(2,1)}, bf16[1,2,256,256]{3,2,1,0:T(8,128)(2,1)}, ...), branch_computations={%region_0.1_spmd, %region_1.2_spmd, %region_2.3_spmd, %region_3.4_... | conditional | bytes 8 | solution.py:379
  2.0 81.2 %gossip_2.1 = (bf16[1,2048,256]{2,1,0:T(8,128)(2,1)S(1)}, bf16[1,2048,256]{2,1,0:T(8,128)(2,1)S(1)}) custom-call(bf16[1,2,32,2048]{3,2,1,0:T(8,128)(2,1)} %get-tuple-element.112.hid, bf16[1,2,256,256]{3,2,1,0:T(8,128)(2,1)} %get-tuple-element.113.qry, bf16[1,2,256,256]{3,2,1,0:T(8,128)(2,1)} %get-tuple-element.114.key, ...), custom_call_target="tpu_custom_call" | custom-call | tf_op jit(solution)/shard_map/cond/branch_2_fun/gossip_2/pallas_call | solution.py:335
  83.4 1.0 %copy.38 = bf16[1,2048,256]{2,1,0:T(8,128)(2,1)} copy(bf16[1,2048,256]{2,1,0:T(8,128)(2,1)S(1)} %get-tuple-element.174) | data formatting | bytes 2097152
  84.4 1.0 %copy.39 = bf16[1,2048,256]{2,1,0:T(8,128)(2,1)} copy(bf16[1,2048,256]{2,1,0:T(8,128)(2,1)S(1)} %get-tuple-element.175) | data formatting | bytes 2097152
Async XLA Ops:
  1.3 0.7 copy-start
  1.3 0.7 copy-start.1
where the time goes:
time: 85.5 us; the launch traced here: 85.4 us
  Pallas kernels  81.2 us (95%)
  local copies, waits for them, and re-layouts  2.62 us (3%)
  between operations  1.32 us (2%)
    pallas_call x1, Pallas kernels, fused(): pl.pallas_call(functools.partial(kernel, bit, (bit + 1) % LEVELS), out_sh...  81.2 us
    unnamed x6, local copies, waits for them, and re-layouts  2.62 us

commit v1 on v0

--- a/solution.py
+++ b/solution.py
@@ -40,11 +40,12 @@
     bit_a, bit_b,
     hid, qry, key, tea, seg, prm, wgt, mom,
     w_out, m_out,
-    x, qv, kv, tv, segv, prmv, wv, mv, stepped, landed, held, att, att_t, live, dvals, total,
+    x, qv, kv, tv, segv, prmv, wv, mv, stepped, landed, held, att, att_t, live, vals, dvals, total,
     load_sem, x_send, x_recv, g_send, g_recv, low_send, low_recv, out_sem,
 ):
-    early = bit_a <= 2
-    lean = bit_a <= 1
+    early = bit_a in (1, 2)
+    paired = bit_b == 0
+    lean = bit_a == 1
     rep = lax.axis_index("rep")
     tp = lax.axis_index("tp")
     row = (tp // 4) * 4
@@ -126,6 +127,13 @@
         for n in range(14):
             hop(s, n).wait_send()
 
+    def loop(first, last, body, unroll=False):
+        def step(i, carry):
+            body(i)
+            return carry
+
+        lax.fori_loop(first, last, step, 0, unroll=unroll)
+
     def attention(s):
         ids = jnp.broadcast_to(segv[pl.ds(s, 1), :].astype(F32), (TOK, TOK))
         ids_t = ids.T
@@ -140,8 +148,9 @@
         alive = jnp.where(place >= prompt, 1.0, 0.0)
         count = jnp.sum(alive, axis=0, keepdims=True)
         live[s] = jnp.broadcast_to(alive / count, (TOK, 128))
-        for h in range(2):
-            cut = pl.ds(h * HEAD_DIM, HEAD_DIM)
+
+        def one_head(h):
+            cut = pl.ds(pl.multiple_of(h * HEAD_DIM, HEAD_DIM), HEAD_DIM)
             scores = lax.dot_general(
                 qv[s, :, cut], kv[s, :, cut], (((1,), (1,)), ((), ())), preferred_element_type=F32
             ) / math.sqrt(HEAD_DIM)
@@ -152,15 +161,24 @@
             att[s, h] = soft.astype(BF16)
             att_t[s, h] = soft.T.astype(BF16)
 
+        loop(0, 2, one_head)
+
     def value_grad(s, values):
-        parts = []
-        for h in range(2):
-            cut = slice(h * HEAD_DIM, (h + 1) * HEAD_DIM)
-            attended = jnp.dot(att[s, h], values[:, cut], preferred_element_type=F32)
+        vals[...] = values
+
+        def one_head(h):
+            cut = pl.ds(pl.multiple_of(h * HEAD_DIM, HEAD_DIM), HEAD_DIM)
+            attended = jnp.dot(att[s, h], vals[:, cut], preferred_element_type=F32)
             residue = attended - tv[s, :, cut].astype(F32)
             errors = (residue * live[s]).astype(BF16)
-            parts.append(jnp.dot(att_t[s, h], errors, preferred_element_type=F32).astype(BF16))
-        return jnp.concatenate(parts, axis=1)
+            dvals[s, :, cut] = jnp.dot(
+                att_t[s, h], errors, preferred_element_type=F32
+            ).astype(BF16)
+
+        loop(0, 2, one_head)
+
+    def rows_of(i):
+        return pl.ds(pl.multiple_of(i * CROWS, CROWS), CROWS)
 
     def send(s, i):
         cut = pl.ds(i * CROWS, CROWS)
@@ -169,23 +187,25 @@
         )
 
     def out_copy(n, i):
-        cut = pl.ds(i * CROWS, CROWS)
+        cut = rows_of(i)
         source, target = ((wv, w_out), (mv, m_out))[n]
         return pltpu.make_async_copy(source.at[cut], target.at[0, cut], out_sem.at[n, i])
-
-    def rows_of(i):
-        return pl.ds(pl.multiple_of(i * CROWS, CROWS), CROWS)
 
     def grad_rows(n, i, dvalues):
         lhs = x[n, :, :, rows_of(i)].reshape(TOK, CROWS)
         return lax.dot_general(lhs, dvalues, (((0,), (0,)), ((), ())), preferred_element_type=F32)
 
-    def update(s, i, target):
+    def moment_rows(s, i):
         cut = rows_of(i)
         moment = (
             MOMENTUM_DECAY * mv[cut, :].astype(F32) + grad_rows(s, i, dvals[s])
         ).astype(BF16)
         mv[cut, :] = moment
+        return moment
+
+    def update(s, i, target):
+        cut = rows_of(i)
+        moment = moment_rows(s, i)
         target[cut, :] = (wv[cut, :].astype(F32) - LEARN_RATE * moment.astype(F32)).astype(BF16)
 
     def average(s, i):
@@ -199,13 +219,6 @@
         total[...] += jnp.dot(
             x[1, :, :, cut].reshape(TOK, count * CROWS), wv[cut, :], preferred_element_type=F32
         )
-
-    def loop(first, last, body):
-        def step(i, carry):
-            body(i)
-            return carry
-
-        lax.fori_loop(first, last, step, 0)
 
     def first_update(i):
         update(0, i, stepped.at[0])
@@ -251,10 +264,117 @@
             hid.at[0, 1], x.at[2, tp], low_send.at[0], low_recv.at[0], peers[1]
         )
         their_grad = remote(dvals.at[1], dvals.at[2], low_send.at[1], low_recv.at[1], peers[1])
+    if paired:
+        their_rows = remote(
+            hid.at[0, 1], x.at[2, tp], low_send.at[0], low_recv.at[0], peers[0]
+        )
+        product = remote(dvals.at[0], dvals.at[2], low_send.at[1], low_recv.at[1], peers[0])
+
+    def paired_steps():
+        quarter = CHUNKS // 2
+        mine = (rep % 2) * quarter
+        other = quarter - mine
+
+        def crossing(n, k):
+            base = (other, mine, other, mine)[n]
+            cut = rows_of(base + k)
+            source, target = (
+                (stepped.at[0], landed.at[0]),
+                (stepped.at[1], landed.at[1]),
+                (mv, held),
+                (wv, landed.at[0]),
+            )[n]
+            m = n // 2 * quarter + k
+            return remote(
+                source.at[cut],
+                target.at[cut],
+                g_send.at[n % 2, m],
+                g_recv.at[n % 2, m],
+                peers[1 - n] if n < 2 else peers[1],
+            )
+
+        def weight_out(k, theirs):
+            cut = rows_of((other if theirs else mine) + k)
+            source = landed.at[0] if theirs else wv
+            sem = out_sem.at[0, k + quarter * theirs]
+            return pltpu.make_async_copy(source.at[cut], w_out.at[0, cut], sem)
+
+        def step_for_mate(k):
+            update(0, other + k, stepped.at[0])
+            crossing(0, k).start()
+
+        def step_for_chip(k):
+            update(0, mine + k, stepped.at[0])
+            cut = rows_of(mine + k)
+            crossing(0, k).wait_recv()
+            both = (stepped[0, cut, :].astype(F32) + landed[0, cut, :].astype(F32)) * 0.5
+            stepped[1, cut, :] = both.astype(BF16)
+            crossing(1, k).start()
+
+        def moment_for_mate(k):
+            moment_rows(1, other + k)
+            crossing(2, k).start()
+            out_copy(1, other + k).start()
+
+        def moment_for_chip(k):
+            moment_rows(1, mine + k)
+            out_copy(1, mine + k).start()
+
+        def weights(k):
+            cut = rows_of(mine + k)
+            crossing(2, k).wait_recv()
+            crossing(1, k).wait_recv()
+            both = stepped[1, cut, :].astype(F32) + landed[1, cut, :].astype(F32)
+            moments = mv[cut, :].astype(F32) + held[cut, :].astype(F32)
+            wv[cut, :] = (both * 0.5 - (0.5 * LEARN_RATE) * moments).astype(BF16)
+            crossing(3, k).start()
+            weight_out(k, False).start()
+
+        def weights_of_mate(k):
+            crossing(3, k).wait_recv()
+            weight_out(k, True).start()
+
+        def end(k):
+            for n in range(4):
+                crossing(n, k).wait_send()
+            weight_out(k, False).wait()
+            weight_out(k, True).wait()
+            out_copy(1, mine + k).wait()
+            out_copy(1, other + k).wait()
+
+        loop(0, quarter, step_for_mate)
+        loop(0, quarter, step_for_chip)
+        stage_b(1)
+        stage_c(1)
+        their_rows.wait_recv()
+        stage_a(2)
+        stage_d(1)
+        total[...] = jnp.dot(
+            x[1].reshape(TOK, ROWS), stepped[0], preferred_element_type=F32
+        )
+        stage_b(2)
+        stage_c(2)
+        stage_d(2)
+        dvals[0] = jnp.dot(
+            x[2].reshape(TOK, ROWS), stepped[0], preferred_element_type=F32
+        ).astype(BF16)
+        product.start()
+        product.wait_recv()
+        values = ((total[...] + dvals[2].astype(F32)) * 0.5).astype(BF16)
+        value_grad(1, values)
+        loop(0, quarter, moment_for_mate)
+        loop(0, quarter, moment_for_chip)
+        loop(0, quarter, weights)
+        loop(0, quarter, weights_of_mate)
+        loop(0, quarter, end)
+        product.wait_send()
+        their_rows.wait_send()
+        for s in range(3):
+            stage_end(s)
 
     own_load[0].wait()
     stage_a(0)
-    if early and bit_b > 1:
+    if early or paired:
         their_rows.start()
     for copy in loads[:5]:
         copy.wait()
@@ -264,8 +384,8 @@
     own_load[1].wait()
     if lean:
         start(1, 2, 3)
-        if bit_b == 1:
-            their_rows.start()
+    elif bit_a == 0:
+        stage_a(1)
     attention(1)
     for copy in loads[5:]:
         copy.wait()
@@ -274,23 +394,27 @@
         start(1, 0, 1, 4, 5)
         their_rows.wait_recv()
         start(2, 2, 3)
-    else:
+    elif bit_a > 0:
         stage_a(1)
 
     values = jnp.dot(
         x[0].reshape(TOK, ROWS), wv[...], preferred_element_type=F32
     ).astype(BF16)
-    dvals[0] = value_grad(0, values)
-    loop(0, CHUNKS, first_update)
+    value_grad(0, values)
+    if paired:
+        paired_steps()
+        return
+    if bit_a == 0:
+        stage_b(1)
+    loop(0, CHUNKS, first_update, bit_a == 0)
     total[...] = jnp.zeros((TOK, COLS), F32)
-    stage_b(1)
     if bit_a == 0:
+        stage_c(1)
         loop(0, CHUNKS, first_gossip)
-        stage_c(1)
         stage_d(1)
-        start(2, 0, 1, 4, 5)
         add_values(0, CHUNKS)
     else:
+        stage_b(1)
         stage_c(1)
         if lean:
             start(2, 0, 1, 4, 5)
@@ -307,18 +431,14 @@
             stage_c(2)
         loop(6, CHUNKS, first_gossip_values)
 
-    dvals[1] = value_grad(1, total[...].astype(BF16))
+    value_grad(1, total[...].astype(BF16))
     if early:
         their_grad.start()
-    if bit_a == 0:
-        stage_b(2)
     loop(0, CHUNKS, second_update)
     if early:
-        if bit_a == 0:
-            stage_c(2)
         stage_d(2)
         their_grad.wait_recv()
-    loop(0, CHUNKS, second_gossip)
+    loop(0, CHUNKS, second_gossip, early)
     loop(0, CHUNKS, finish)
     stage_end(0)
     stage_end(1)
@@ -355,6 +475,7 @@
             pltpu.VMEM((2, 2, TOK, TOK), BF16),
             pltpu.VMEM((2, 2, TOK, TOK), BF16),
             pltpu.VMEM((2, TOK, 128), F32),
+            pltpu.VMEM((TOK, COLS), BF16),
             pltpu.VMEM((3, TOK, COLS), BF16),
             pltpu.VMEM((TOK, COLS), F32),
             dma((9,)),

time: 85.5 us -> 55.6 us (0.65)
  the two profiles are of different devices: /device:TPU:128 before, /device:TPU:8 now
where the time goes in v1:
time: 55.6 us; the launch traced here: 55.4 us
  Pallas kernels  51.3 us (92%)
  local copies, waits for them, and re-layouts  2.62 us (5%)
  between operations  1.32 us (2%)
    pallas_call x1, Pallas kernels, fused(): pl.pallas_call(functools.partial(kernel, bit, (bit + 1) % LEVELS), out_sh...  51.3 us
    unnamed x6, local copies, waits for them, and re-layouts  2.62 us

profile of v1, /device:TPU:8, one launch (start us, length us, event | category | flops | bytes accessed | tf_op | source)
XLA Modules:
  0.0 55.4 jit_solution(7188703606307519526)
XLA Ops:
  1.3 0.0 copy-start
  1.3 0.0 copy-start.1
  1.3 0.7 %copy-done = s32[1,2,256]{2,1,0:T(2,128)S(1)} copy-done((s32[1,2,256]{2,1,0:T(2,128)S(1)}, s32[1,2,256]{2,1,0:T(2,128)}, u32[]{:S(2)}) %copy-start) | copy-done | bytes 2072
  2.0 0.0 copy-done.1
  2.0 51.5 %conditional.1 = ((bf16[1,2048,256]{2,1,0:T(8,128)(2,1)S(1)}, bf16[1,2048,256]{2,1,0:T(8,128)(2,1)S(1)})) conditional(s32[]{:T(128)} %clamp.3, (bf16[1,2,32,2048]{3,2,1,0:T(8,128)(2,1)}, bf16[1,2,256,256]{3,2,1,0:T(8,128)(2,1)}, bf16[1,2,256,256]{3,2,1,0:T(8,128)(2,1)}, bf16[1,2,256,256]{3,2,1,0:T(8,128)(2,1)}, ...), branch_computations={%region_0.1_spmd, %region_1.2_spmd, %region_2.3_spmd, %region_3.4_... | conditional | bytes 8 | solution.py:500
  2.0 51.3 %gossip_0.1 = (bf16[1,2048,256]{2,1,0:T(8,128)(2,1)S(1)}, bf16[1,2048,256]{2,1,0:T(8,128)(2,1)S(1)}) custom-call(bf16[1,2,32,2048]{3,2,1,0:T(8,128)(2,1)} %get-tuple-element.96.hid, bf16[1,2,256,256]{3,2,1,0:T(8,128)(2,1)} %get-tuple-element.97.qry, bf16[1,2,256,256]{3,2,1,0:T(8,128)(2,1)} %get-tuple-element.98.key, ...), custom_call_target="tpu_custom_call" | custom-call | tf_op jit(solution)/shard_map/cond/branch_0_fun/gossip_0/pallas_call | solution.py:455
  53.5 1.0 %copy.38 = bf16[1,2048,256]{2,1,0:T(8,128)(2,1)} copy(bf16[1,2048,256]{2,1,0:T(8,128)(2,1)S(1)} %get-tuple-element.174) | data formatting | bytes 2097152
  54.5 1.0 %copy.39 = bf16[1,2048,256]{2,1,0:T(8,128)(2,1)} copy(bf16[1,2048,256]{2,1,0:T(8,128)(2,1)S(1)} %get-tuple-element.175) | data formatting | bytes 2097152
Async XLA Ops:
  1.3 0.7 %copy-start = (s32[1,2,256]{2,1,0:T(2,128)S(1)}, s32[1,2,256]{2,1,0:T(2,128)}, u32[]{:S(2)}) copy-start(s32[1,2,256]{2,1,0:T(2,128)} %param.19) | copy-start | bytes 6148
  1.3 0.7 %copy-start.1 = (s32[1,2,8]{2,1,0:T(2,128)S(1)}, s32[1,2,8]{2,1,0:T(2,128)}, u32[]{:S(2)}) copy-start(s32[1,2,8]{2,1,0:T(2,128)} %param.20) | copy-start | bytes 196

commit v2 on v1

--- a/solution.py
+++ b/solution.py
@@ -12,6 +12,7 @@
 LEARN_RATE = 0.1
 MOMENTUM_DECAY = 0.9
 LEVELS = 6
+REPS = 1 << LEVELS
 TOK = 256
 ROWS = 2048
 COLS = 256
@@ -45,6 +46,7 @@
 ):
     early = bit_a in (1, 2)
     paired = bit_b == 0
+    ring = bit_a == 4
     lean = bit_a == 1
     rep = lax.axis_index("rep")
     tp = lax.axis_index("tp")
@@ -58,7 +60,10 @@
     to_right = (rep, right)
     to_left = (rep, left)
     to_cross = (rep, cross)
-    peers = ((partner_of(rep, bit_a), tp), (partner_of(rep, bit_b), tp))
+    partner = (partner_of(rep, bit_a), tp)
+    peers = (partner, (partner_of(rep, bit_b), tp))
+    if ring:
+        peers = (((rep + (1 << bit_a)) % REPS, tp), ((rep + REPS - (1 << bit_a)) % REPS, tp))
 
     own_load = [pltpu.make_async_copy(hid.at[0, s], x.at[s, tp], load_sem.at[s]) for s in range(2)]
     loads = [
@@ -127,12 +132,12 @@
         for n in range(14):
             hop(s, n).wait_send()
 
-    def loop(first, last, body, unroll=False):
+    def loop(first, last, body):
         def step(i, carry):
             body(i)
             return carry
 
-        lax.fori_loop(first, last, step, 0, unroll=unroll)
+        lax.fori_loop(first, last, step, 0)
 
     def attention(s):
         ids = jnp.broadcast_to(segv[pl.ds(s, 1), :].astype(F32), (TOK, TOK))
@@ -224,6 +229,10 @@
         update(0, i, stepped.at[0])
         send(0, i).start()
 
+    def first_updates(k):
+        first_update(2 * k)
+        first_update(2 * k + 1)
+
     def first_gossip(i):
         average(0, i)
         if early:
@@ -264,11 +273,107 @@
             hid.at[0, 1], x.at[2, tp], low_send.at[0], low_recv.at[0], peers[1]
         )
         their_grad = remote(dvals.at[1], dvals.at[2], low_send.at[1], low_recv.at[1], peers[1])
-    if paired:
+    if paired or ring:
         their_rows = remote(
-            hid.at[0, 1], x.at[2, tp], low_send.at[0], low_recv.at[0], peers[0]
+            hid.at[0, 1], x.at[2, tp], low_send.at[0], low_recv.at[0], partner
         )
-        product = remote(dvals.at[0], dvals.at[2], low_send.at[1], low_recv.at[1], peers[0])
+        product = remote(dvals.at[0], dvals.at[2], low_send.at[1], low_recv.at[1], partner)
+
+    def partner_values(between):
+        stage_b(1)
+        stage_c(1)
+        their_rows.wait_recv()
+        stage_a(2)
+        stage_d(1)
+        total[...] = jnp.dot(
+            x[1].reshape(TOK, ROWS), stepped[0], preferred_element_type=F32
+        )
+        stage_b(2)
+        stage_c(2)
+        stage_d(2)
+        dvals[0] = jnp.dot(
+            x[2].reshape(TOK, ROWS), stepped[0], preferred_element_type=F32
+        ).astype(BF16)
+        product.start()
+        between()
+        product.wait_recv()
+        values = ((total[...] + dvals[2].astype(F32)) * 0.5).astype(BF16)
+        value_grad(1, values)
+
+    def partner_end():
+        product.wait_send()
+        their_rows.wait_send()
+        for s in range(3):
+            stage_end(s)
+
+    def ring_steps():
+        half = CHUNKS // 2
+
+        def both(k, body):
+            body(k, 0)
+            body(half + k, 1)
+
+        def passing(n, i, way):
+            cut = rows_of(i)
+            source = (stepped.at[0], stepped.at[1], held)[n]
+            device = peers[1 - way if n == 0 else way]
+            return remote(
+                source.at[cut], landed.at[n, cut], g_send.at[n, i], g_recv.at[n, i], device
+            )
+
+        def step(i, way):
+            update(0, i, stepped.at[0])
+
+        def pass_step(i, way):
+            passing(0, i, way).start()
+
+        def second(i, way):
+            cut = rows_of(i)
+            moment = moment_rows(1, i)
+            out_copy(1, i).start()
+            stepped[1, cut, :] = (
+                stepped[0, cut, :].astype(F32) - (2 * LEARN_RATE) * moment.astype(F32)
+            ).astype(BF16)
+            passing(1, i, way).start()
+
+        def relay(i, way):
+            cut = rows_of(i)
+            passing(1, i, way).wait_recv()
+            held[cut, :] = (
+                landed[1, cut, :].astype(F32) + stepped[0, cut, :].astype(F32)
+            ).astype(BF16)
+            passing(2, i, way).start()
+
+        def weights(i, way):
+            cut = rows_of(i)
+            passing(0, i, way).wait_recv()
+            passing(2, i, way).wait_recv()
+            own = stepped[0, cut, :].astype(F32) - (2 * LEARN_RATE) * mv[cut, :].astype(F32)
+            theirs = landed[0, cut, :].astype(F32) + landed[2, cut, :].astype(F32)
+            wv[cut, :] = ((own + theirs) * 0.25).astype(BF16)
+            out_copy(0, i).start()
+
+        def end(i, way):
+            for n in range(3):
+                passing(n, i, way).wait_send()
+            out_copy(0, i).wait()
+            out_copy(1, i).wait()
+
+        def each(first, last, *bodies):
+            def step_both(k):
+                for body in bodies:
+                    both(k, body)
+
+            loop(first, last, step_both)
+
+        each(0, 2, step, pass_step)
+        each(2, half, step)
+        partner_values(lambda: each(2, half, pass_step))
+        each(0, half, second)
+        each(0, half, relay)
+        each(0, half, weights)
+        each(0, half, end)
+        partner_end()
 
     def paired_steps():
         quarter = CHUNKS // 2
@@ -344,37 +449,17 @@
 
         loop(0, quarter, step_for_mate)
         loop(0, quarter, step_for_chip)
-        stage_b(1)
-        stage_c(1)
-        their_rows.wait_recv()
-        stage_a(2)
-        stage_d(1)
-        total[...] = jnp.dot(
-            x[1].reshape(TOK, ROWS), stepped[0], preferred_element_type=F32
-        )
-        stage_b(2)
-        stage_c(2)
-        stage_d(2)
-        dvals[0] = jnp.dot(
-            x[2].reshape(TOK, ROWS), stepped[0], preferred_element_type=F32
-        ).astype(BF16)
-        product.start()
-        product.wait_recv()
-        values = ((total[...] + dvals[2].astype(F32)) * 0.5).astype(BF16)
-        value_grad(1, values)
+        partner_values(lambda: None)
         loop(0, quarter, moment_for_mate)
         loop(0, quarter, moment_for_chip)
         loop(0, quarter, weights)
         loop(0, quarter, weights_of_mate)
         loop(0, quarter, end)
-        product.wait_send()
-        their_rows.wait_send()
-        for s in range(3):
-            stage_end(s)
+        partner_end()
 
     own_load[0].wait()
     stage_a(0)
-    if early or paired:
+    if early or paired or ring:
         their_rows.start()
     for copy in loads[:5]:
         copy.wait()
@@ -404,9 +489,15 @@
     if paired:
         paired_steps()
         return
+    if ring:
+        ring_steps()
+        return
     if bit_a == 0:
         stage_b(1)
-    loop(0, CHUNKS, first_update, bit_a == 0)
+    if bit_a == 0:
+        loop(0, CHUNKS // 2, first_updates)
+    else:
+        loop(0, CHUNKS, first_update)
     total[...] = jnp.zeros((TOK, COLS), F32)
     if bit_a == 0:
         stage_c(1)
@@ -438,7 +529,7 @@
     if early:
         stage_d(2)
         their_grad.wait_recv()
-    loop(0, CHUNKS, second_gossip, early)
+    loop(0, CHUNKS, second_gossip)
     loop(0, CHUNKS, finish)
     stage_end(0)
     stage_end(1)
@@ -470,7 +561,7 @@
             pltpu.VMEM((ROWS, COLS), BF16),
             pltpu.VMEM((ROWS, COLS), BF16),
             pltpu.VMEM((2, ROWS, COLS), BF16),
-            pltpu.VMEM((2, ROWS, COLS), BF16),
+            pltpu.VMEM((3, ROWS, COLS), BF16),
             pltpu.VMEM((ROWS, COLS), BF16),
             pltpu.VMEM((2, 2, TOK, TOK), BF16),
             pltpu.VMEM((2, 2, TOK, TOK), BF16),
@@ -481,8 +572,8 @@
             dma((9,)),
             dma((3, 14)),
             dma((3, 14)),
-            dma((2, CHUNKS)),
-            dma((2, CHUNKS)),
+            dma((3, CHUNKS)),
+            dma((3, CHUNKS)),
             dma((2,)),
             dma((2,)),
             dma((2, CHUNKS)),

time: 55.6 us -> 186 us (3.35)
  the two profiles are of different devices: /device:TPU:8 before, /device:TPU:3 now
where the time goes in v2:
time: 186 us
  Pallas kernels  182 us (98%)
  local copies, waits for them, and re-layouts  2.62 us (1%)
    pallas_call x1, Pallas kernels, fused(): pl.pallas_call(functools.partial(kernel, bit, (bit + 1) % LEVELS), out_sh...  182 us

profile of v2, /device:TPU:3, one launch (start us, length us, event | category | flops | bytes accessed | tf_op | source)
XLA Modules:
  0.0 185.9 jit_solution(8846464830135609977)
XLA Ops:
  1.3 0.0 copy-start
  1.3 0.0 copy-start.1
  1.3 0.7 copy-done
  2.0 0.0 copy-done.1
  2.0 182.0 %conditional.1 = ((bf16[1,2048,256]{2,1,0:T(8,128)(2,1)S(1)}, bf16[1,2048,256]{2,1,0:T(8,128)(2,1)S(1)})) conditional(s32[]{:T(128)} %clamp.3, (bf16[1,2,32,2048]{3,2,1,0:T(8,128)(2,1)}, bf16[1,2,256,256]{3,2,1,0:T(8,128)(2,1)}, bf16[1,2,256,256]{3,2,1,0:T(8,128)(2,1)}, bf16[1,2,256,256]{3,2,1,0:T(8,128)(2,1)}, ...), branch_computations={%region_0.1_spmd, %region_1.2_spmd, %region_2.3_spmd, %region_3.4_... | conditional | bytes 8 | solution.py:591
  2.0 181.8 %gossip_4.1 = (bf16[1,2048,256]{2,1,0:T(8,128)(2,1)S(1)}, bf16[1,2048,256]{2,1,0:T(8,128)(2,1)S(1)}) custom-call(bf16[1,2,32,2048]{3,2,1,0:T(8,128)(2,1)} %get-tuple-element.128.hid, bf16[1,2,256,256]{3,2,1,0:T(8,128)(2,1)} %get-tuple-element.129.qry, bf16[1,2,256,256]{3,2,1,0:T(8,128)(2,1)} %get-tuple-element.130.key, ...), custom_call_target="tpu_custom_call" | custom-call | tf_op jit(solution)/shard_map/cond/branch_4_fun/gossip_4/pallas_call | solution.py:546
  184.0 1.0 copy.38
  185.0 1.0 copy.39
Async XLA Ops:
  1.3 0.7 copy-start
  1.3 0.7 copy-start.1

commit v3 on v2

--- a/solution.py
+++ b/solution.py
@@ -44,7 +44,7 @@
     x, qv, kv, tv, segv, prmv, wv, mv, stepped, landed, held, att, att_t, live, vals, dvals, total,
     load_sem, x_send, x_recv, g_send, g_recv, low_send, low_recv, out_sem,
 ):
-    early = bit_a in (1, 2)
+    early = bit_a in (1, 2, 3)
     paired = bit_b == 0
     ring = bit_a == 4
     lean = bit_a == 1
@@ -461,9 +461,6 @@
     stage_a(0)
     if early or paired or ring:
         their_rows.start()
-    for copy in loads[:5]:
-        copy.wait()
-    attention(0)
     stage_b(0)
     stage_c(0)
     own_load[1].wait()
@@ -471,9 +468,9 @@
         start(1, 2, 3)
     elif bit_a == 0:
         stage_a(1)
-    attention(1)
-    for copy in loads[5:]:
+    for copy in loads:
         copy.wait()
+    loop(0, 2, attention)
     stage_d(0)
     if lean:
         start(1, 0, 1, 4, 5)

time: 186 us -> 102 us (0.55)
  the two profiles are of different devices: /device:TPU:3 before, /device:TPU:33 now
where the time goes in v3:
time: 102 us
  Pallas kernels  98.1 us (96%)
  local copies, waits for them, and re-layouts  2.62 us (3%)
  between operations  1.32 us (1%)
    pallas_call x1, Pallas kernels, fused(): pl.pallas_call(functools.partial(kernel, bit, (bit + 1) % LEVELS), out_sh...  98.1 us
    unnamed x6, local copies, waits for them, and re-layouts  2.62 us

profile of v3, /device:TPU:33, one launch (start us, length us, event | category | flops | bytes accessed | tf_op | source)
XLA Modules:
  0.0 102.2 jit_solution(14915255468979346728)
XLA Ops:
  1.3 0.0 copy-start
  1.3 0.0 copy-start.1
  1.3 0.7 copy-done
  2.0 0.0 copy-done.1
  2.0 98.3 %conditional.1 = ((bf16[1,2048,256]{2,1,0:T(8,128)(2,1)S(1)}, bf16[1,2048,256]{2,1,0:T(8,128)(2,1)S(1)})) conditional(s32[]{:T(128)} %clamp.3, (bf16[1,2,32,2048]{3,2,1,0:T(8,128)(2,1)}, bf16[1,2,256,256]{3,2,1,0:T(8,128)(2,1)}, bf16[1,2,256,256]{3,2,1,0:T(8,128)(2,1)}, bf16[1,2,256,256]{3,2,1,0:T(8,128)(2,1)}, ...), branch_computations={%region_0.1_spmd, %region_1.2_spmd, %region_2.3_spmd, %region_3.4_... | conditional | bytes 8 | solution.py:588
  2.0 98.1 %gossip_5.1 = (bf16[1,2048,256]{2,1,0:T(8,128)(2,1)S(1)}, bf16[1,2048,256]{2,1,0:T(8,128)(2,1)S(1)}) custom-call(bf16[1,2,32,2048]{3,2,1,0:T(8,128)(2,1)} %get-tuple-element.136.hid, bf16[1,2,256,256]{3,2,1,0:T(8,128)(2,1)} %get-tuple-element.137.qry, bf16[1,2,256,256]{3,2,1,0:T(8,128)(2,1)} %get-tuple-element.138.key, ...), custom_call_target="tpu_custom_call" | custom-call | tf_op jit(solution)/shard_map/cond/branch_5_fun/gossip_5/pallas_call | solution.py:543
  100.3 1.0 copy.38
  101.2 1.0 copy.39
Async XLA Ops:
  1.3 0.7 copy-start
  1.3 0.7 copy-start.1
